TPU v7x, 256 devices: a whole 4x4x8 slice. The times are simulated.
256 devices in a mesh: section: 4 (over x), fsdp: 64 (over y, z, core).
Axes of the slice: x: 4, y: 4, z: 8, core: 2. Of those that a mesh axis runs over, the one named last changes fastest.
Arguments:
- enc_states: bfloat16 [64, 4, 1280], P('fsdp'), may hold values from -6 to 6
- clip_frames: int32 [64], replicated, may hold values from 2 to 4, as said below
- clip_offset: int32 [64], replicated, may hold values from 0 to 126, as said below
- ln_gain: float32 [1280], replicated, may hold values from 0.1 to 1.9
- ln_bias: float32 [1280], replicated, may hold values from -0.6 to 0.6
- w_proj: bfloat16 [1280, 8192], P(None, 'fsdp'), may hold values from -0.15625 to 0.15625
- proj_bias: float32 [8192], P('fsdp'), may hold values from -3 to 3
- text_embed: bfloat16 [64, 2, 8192], P(None, None, 'fsdp'), may hold values from -6 to 6
- norm_gain: float32 [4, 8192], P('section'), may hold values from 0.1 to 1.9
- w_gate: bfloat16 [4, 14784, 8192], P('section', 'fsdp'), may hold values from -0.0625 to 0.0625
- w_up: bfloat16 [4, 14784, 8192], P('section', 'fsdp'), may hold values from -0.0625 to 0.0625
- w_down: bfloat16 [4, 14784, 8192], P('section', 'fsdp'), may hold values from -0.046875 to 0.046875
Outputs:
- stream_out: bfloat16 [64, 2, 8192], P('section', None, 'fsdp')
Inputs may be any that keep to these rules, and one draw needn't show every extreme that they name: `clip_frames`: every clip's frame count is even, and some clip has exactly 4 frames. Clip c's live rows occupy stream positions clip_offset[c] to clip_offset[c] + clip_frames[c] / 2 - 1, all inside one microbatch (positions m * 64 to (m + 1) * 64 - 1); no two clips share a position; each microbatch holds 32 clips.
All inputs are finite; a program needn't handle non-finite values.
Results may differ from a plain program's by a relative error of at most 0.015.
Values may be sent and summed in bfloat16 or wider, within the bound.
A program may use at most 64 MiB of HBM per device.

v0:
```python
import jax
import jax.numpy as jnp
from jax import lax
from jax.sharding import PartitionSpec as P


def from_behind(value, axis, steps):
    count = lax.axis_size(axis)
    initial, last = (max(0, -steps), min(count, count - steps))
    return lax.ppermute(value, axis, [(source, source + steps) for source in range(initial, last)])


def from_root(value, axis, source):
    kept = jnp.where(lax.axis_index(axis) == source, value, 0).astype(value.dtype)
    return lax.psum(kept, axis)


def rms_scaled(stream, gain):
    values = stream.astype(jnp.float32)
    scale = lax.rsqrt(jnp.mean(values * values, axis=-1, keepdims=True) + 1e-06)
    return (values * scale * gain).astype(jnp.bfloat16)


def on_device(
    enc_states,
    clip_frames,
    clip_offset,
    ln_gain,
    ln_bias,
    w_proj,
    proj_bias,
    text_embed,
    norm_gain,
    w_gate,
    w_up,
    w_down,
):
    section_count = lax.axis_size("section")
    section_index = lax.axis_index("section")
    local_clips, frame_len, enc_width = enc_states.shape
    clip_rows = frame_len // 2
    tokens, micro, feat_local = text_embed.shape
    slots = tokens * micro
    pairs = enc_states.astype(jnp.float32).reshape(local_clips, clip_rows, 2, enc_width)
    pooled = 0.5 * (pairs[:, :, 0] + pairs[:, :, 1])
    centre = jnp.mean(pooled, axis=-1, keepdims=True)
    centred = pooled - centre
    spread = jnp.mean(centred * centred, axis=-1, keepdims=True)
    audio_ln = (centred * lax.rsqrt(spread + 1e-05) * ln_gain + ln_bias).astype(jnp.bfloat16)
    audio_ln = audio_ln.reshape(local_clips * clip_rows, enc_width)
    summed = jnp.dot(
        lax.all_gather(audio_ln, "fsdp", axis=0, tiled=True),
        w_proj,
        preferred_element_type=jnp.float32,
    )
    projected = (summed + proj_bias).astype(jnp.bfloat16)
    within = jnp.arange(clip_rows, dtype=jnp.int32)
    live = within[None, :] * 2 < clip_frames[:, None]
    spot = clip_offset[:, None] + within[None, :]
    target = jnp.where(live, spot % tokens * micro + spot // tokens, slots).reshape(-1)
    flags = jnp.zeros((slots,), jnp.int32).at[target].set(1, mode="drop").reshape(tokens, micro)
    placed = jnp.zeros((slots, feat_local), jnp.bfloat16).at[target].set(projected, mode="drop")
    placed = placed.reshape(tokens, micro, feat_local)
    embedded = jnp.where(flags[:, :, None] == 1, placed, text_embed)
    gain = norm_gain[0]
    gate_w = w_gate[0]
    up_w = w_up[0]
    down_w = w_down[0]
    width = gate_w.shape[1]
    dims = (((1,), (1,)), ((), ()))
    waves = micro // micro
    turns = waves + section_count - 1
    zero_rows = jnp.zeros((tokens, micro, feat_local), jnp.bfloat16)
    incoming = zero_rows
    finished = jnp.zeros((tokens, micro, feat_local), jnp.bfloat16)
    first_section = section_index == 0
    for turn in range(turns):
        if turn < waves:
            fresh = embedded
        else:
            fresh = zero_rows
        current = jnp.where(first_section, fresh, incoming)
        whole = lax.all_gather(current, "fsdp", axis=2, tiled=True)
        layer_normed = rms_scaled(whole, gain).reshape(-1, width)
        gate = lax.dot_general(layer_normed, gate_w, dims, preferred_element_type=jnp.float32)
        up = lax.dot_general(layer_normed, up_w, dims, preferred_element_type=jnp.float32)
        hidden = (jax.nn.silu(gate) * up).astype(jnp.bfloat16)
        partial_sum = jnp.dot(hidden, down_w, preferred_element_type=jnp.float32).reshape(
            tokens, micro, width
        )
        branch = lax.psum_scatter(partial_sum, "fsdp", scatter_dimension=2, tiled=True)
        output = (current.astype(jnp.float32) + branch).astype(jnp.bfloat16)
        leaving = turn - (section_count - 1)
        if leaving >= 0:
            finished = finished.at[:, leaving * micro : (leaving + 1) * micro].set(output)
        if turn + 1 < turns:
            incoming = from_behind(output, "section", 1)
    complete = from_root(finished, "section", section_count - 1)
    rows_each = tokens // section_count
    return lax.dynamic_slice_in_dim(complete, section_index * rows_each, rows_each, 0)


def solution(mesh):
    placed = (
        P("fsdp", None, None),
        P(),
        P(),
        P(),
        P(),
        P(None, "fsdp"),
        P("fsdp"),
        P(None, None, "fsdp"),
        P("section", None),
        P("section", "fsdp", None),
        P("section", "fsdp", None),
        P("section", "fsdp", None),
    )
    return jax.shard_map(
        on_device, mesh=mesh, in_specs=placed, out_specs=P("section", None, "fsdp"), check_vma=False
    )
```

profile of v0, /device:TPU:8, one launch (start us, length us, event | category | flops | bytes accessed | tf_op | source)
XLA Modules:
  0.0 1049.0 jit_solution(15921234189649798289)
XLA Ops:
  8.4 50.3 %all-gather = bf16[64,2,1280]{2,1,0:T(2,128)(2,1)S(1)} all-gather(bf16[1,2,1280]{2,1,0:T(2,128)(2,1)S(1)} %fusion.76), channel_id=1, replica_groups=mesh['section'=4,'fsdp'=64] {'fsdp'}, dimensions={0}, use_global_device_ids=true | all-gather | bytes 332800 | tf_op jit(solution)/shard_map/all_gather | solution.py:52
  65.2 71.5 %all-gather.6.cloned.1.call-done = bf16[64,2,8192]{2,0,1:T(8,128)(2,1)} async-done(((bf16[64,2,128]{2,0,1:T(8,128)(2,1)}), bf16[64,2,8192]{2,0,1:T(8,128)(2,1)}) %all-gather.6.cloned.1.call-update) | async-done | bytes 2097168 | tf_op jit(solution)/shard_map/all_gather | solution.py:83
  141.0 3.5 copy.55
  147.3 3.5 fusion.34
  152.2 4.8 fusion.18
  157.1 141.9 %reduce-scatter.5.cloned.1.call-done = f32[64,2,128]{2,0,1:T(8,128)} async-done(((f32[64,2,8192]{2,0,1:T(8,128)}), f32[64,2,128]{2,0,1:T(8,128)}) %reduce-scatter.5.cloned.1.call-update) | async-done | bytes 65552 | tf_op jit(solution)/shard_map/reduce_scatter | solution.py:91
  299.9 3.4 collective-permute-start
  305.7 72.4 %all-gather.8.cloned.1.call-done = bf16[64,2,8192]{2,0,1:T(8,128)(2,1)} async-done(((bf16[64,2,128]{2,0,1:T(8,128)(2,1)}), bf16[64,2,8192]{2,0,1:T(8,128)(2,1)}) %all-gather.8.cloned.1.call-update) | async-done | bytes 2097168 | tf_op jit(solution)/shard_map/all_gather | solution.py:83
  382.4 3.5 copy.58
  388.7 3.5 fusion.32
  393.7 4.8 fusion.16
  398.6 142.0 %reduce-scatter.7.cloned.1.call-done = f32[64,2,128]{2,0,1:T(8,128)} async-done(((f32[64,2,8192]{2,0,1:T(8,128)}), f32[64,2,128]{2,0,1:T(8,128)}) %reduce-scatter.7.cloned.1.call-update) | async-done | bytes 65552 | tf_op jit(solution)/shard_map/reduce_scatter | solution.py:91
  541.5 3.3 collective-permute-start.1
  547.3 72.4 %all-gather.10.cloned.1.call-done = bf16[64,2,8192]{2,0,1:T(8,128)(2,1)} async-done(((bf16[64,2,128]{2,0,1:T(8,128)(2,1)}), bf16[64,2,8192]{2,0,1:T(8,128)(2,1)}) %all-gather.10.cloned.1.call-update) | async-done | bytes 2097168 | tf_op jit(solution)/shard_map/all_gather | solution.py:83
  624.0 3.5 copy.61
  630.3 3.4 fusion.30
  635.3 4.8 fusion.14
  640.2 142.1 %reduce-scatter.9.cloned.1.call-done = f32[64,2,128]{2,0,1:T(8,128)} async-done(((f32[64,2,8192]{2,0,1:T(8,128)}), f32[64,2,128]{2,0,1:T(8,128)}) %reduce-scatter.9.cloned.1.call-update) | async-done | bytes 65552 | tf_op jit(solution)/shard_map/reduce_scatter | solution.py:91
  788.9 72.3 %all-gather.12.cloned.1.call-done = bf16[64,2,8192]{2,0,1:T(8,128)(2,1)} async-done(((bf16[64,2,128]{2,0,1:T(8,128)(2,1)}), bf16[64,2,8192]{2,0,1:T(8,128)(2,1)}) %all-gather.12.cloned.1.call-update) | async-done | bytes 2097168 | tf_op jit(solution)/shard_map/all_gather | solution.py:83
  865.5 3.5 copy.64
  871.8 3.5 fusion.28
  876.8 4.8 fusion.12
  881.6 142.0 %reduce-scatter.11.cloned.1.call-done = f32[64,2,128]{2,0,1:T(8,128)} async-done(((f32[64,2,8192]{2,0,1:T(8,128)}), f32[64,2,128]{2,0,1:T(8,128)}) %reduce-scatter.11.cloned.1.call-update) | async-done | bytes 65552 | tf_op jit(solution)/shard_map/reduce_scatter | solution.py:91
  1024.5 17.0 %psum.7 = bf16[64,2,128]{2,0,1:T(8,128)(2,1)S(1)} all-reduce(bf16[64,2,128]{2,0,1:T(8,128)(2,1)S(1)} %fusion.65), channel_id=1, replica_groups=mesh['section'=4,'fsdp'=64] {'section'}, use_global_device_ids=true, to_apply=%region_12.13 | all-reduce | flops 16384 | bytes 65536 | tf_op jit(solution)/shard_map/psum | solution.py:15
  (92 shorter events, 57.2 us)
Async XLA Ops:
  6.5 55.3 %copy-start = (bf16[1280,128]{1,0:T(8,128)(2,1)S(1)}, bf16[1280,128]{1,0:T(8,128)(2,1)}, u32[]{:S(2)}) copy-start(bf16[1280,128]{1,0:T(8,128)(2,1)} %param.21) | copy-start | bytes 983044
  6.5 132.3 %copy-start.5 = (f32[1,8192]{1,0:T(1,128)S(1)}, f32[1,8192]{1,0:T(1,128)}, u32[]{:S(2)}) copy-start(f32[1,8192]{1,0:T(1,128)} %param.24) | copy-start | bytes 98308
  6.5 130.1 %all-gather.6.cloned.1.call-start = ((), (), s32[]{:S(2)}) async-start(), calls=%async_computation.4 | async-start | bytes 2129920 | tf_op jit(solution)/shard_map/all_gather | solution.py:83
  65.2 233.9 %reduce-scatter.5.cloned.1.call-start = ((), (), s32[]{:S(2)}) async-start(), calls=%async_computation.5 | async-start | bytes 4259840 | tf_op jit(solution)/shard_map/reduce_scatter | solution.py:91
  147.3 3.5 copy-start.1
  157.0 142.0 %copy-start.6 = (bf16[64,2,128]{2,0,1:T(8,128)(2,1)S(1)}, bf16[64,2,128]{2,0,1:T(8,128)(2,1)}, u32[]{:S(2)}) copy-start(bf16[64,2,128]{2,0,1:T(8,128)(2,1)} %fusion.66) | copy-start | bytes 98308
  157.1 221.1 %all-gather.8.cloned.1.call-start = ((), (), s32[]{:S(2)}) async-start(), calls=%async_computation.6 | async-start | bytes 2129920 | tf_op jit(solution)/shard_map/all_gather | solution.py:83
  299.9 5.0 collective-permute-start
  305.5 235.1 %reduce-scatter.7.cloned.1.call-start = ((), (), s32[]{:S(2)}) async-start(), calls=%async_computation.7 | async-start | bytes 4259840 | tf_op jit(solution)/shard_map/reduce_scatter | solution.py:91
  388.7 3.5 copy-start.2
  398.5 221.2 %all-gather.10.cloned.1.call-start = ((), (), s32[]{:S(2)}) async-start(), calls=%async_computation.8 | async-start | bytes 2129920 | tf_op jit(solution)/shard_map/all_gather | solution.py:83
  541.5 4.9 collective-permute-start.1
  547.0 235.2 %reduce-scatter.9.cloned.1.call-start = ((), (), s32[]{:S(2)}) async-start(), calls=%async_computation.9 | async-start | bytes 4259840 | tf_op jit(solution)/shard_map/reduce_scatter | solution.py:91
  630.3 3.5 copy-start.3
  640.1 221.1 %all-gather.12.cloned.1.call-start = ((), (), s32[]{:S(2)}) async-start(), calls=%async_computation.10 | async-start | bytes 2129920 | tf_op jit(solution)/shard_map/all_gather | solution.py:83
  783.1 4.9 collective-permute-start.2
  788.6 235.0 %reduce-scatter.11.cloned.1.call-start = ((), (), s32[]{:S(2)}) async-start(), calls=%async_computation.11 | async-start | bytes 4259840 | tf_op jit(solution)/shard_map/reduce_scatter | solution.py:91
  871.8 3.5 copy-start.4
Sparse Core Ops, SparseCore 0:
  65.3 71.3 all-gather.5
  157.2 141.8 reduce-scatter.4
  305.6 72.5 all-gather.7
  398.7 141.9 reduce-scatter.6
  547.1 72.5 all-gather.9
  640.2 141.9 reduce-scatter.8
  788.7 72.4 all-gather.11
  881.7 141.8 reduce-scatter.10
where the time goes:
time: 1050 us
  waiting for transfers between devices  862 us (82%)
  blocking collectives  67.3 us (6%)
  matrix products  39.3 us (4%)
  local copies, waits for them, and re-layouts  29.6 us (3%)
  other arithmetic  26.4 us (3%)
  between operations  13.9 us (1%)
  starting transfers between devices  10.9 us (1%)
    reduce_scatter x4, waiting for transfers between devices, on_device(): lax.psum_scatter(partial_sum, 'fsdp', scatter_dimension=2, tiled=True)  568 us
    all_gather x4, waiting for transfers between devices, on_device(): whole = lax.all_gather(current, 'fsdp', axis=2, tiled=True)  289 us
    all_gather x1, blocking collectives, on_device(): lax.all_gather(audio_ln, 'fsdp', axis=0, tiled=True)  50.3 us
  transfers between devices with their start and end apart: 11, of which 11 were waited for; matrix products, arithmetic and copies ran while one was open for 0% of the time, Pallas kernels for 0%

commit v1 on v0

--- a/solution.py
+++ b/solution.py
@@ -80,7 +80,17 @@
         else:
             fresh = zero_rows
         current = jnp.where(first_section, fresh, incoming)
-        whole = lax.all_gather(current, "fsdp", axis=2, tiled=True)
+
+        def open_sectors_for(which_dim, my_tile):
+            vec_out = lax.all_to_all(
+                jnp.stack(lax.axis_size("fsdp") * [my_tile], axis=0),
+                axis_name="fsdp",
+                split_axis=0,
+                concat_axis=0,
+            )
+            return jnp.concatenate(vec_out, axis=which_dim)
+
+        whole = open_sectors_for(2, current)
         layer_normed = rms_scaled(whole, gain).reshape(-1, width)
         gate = lax.dot_general(layer_normed, gate_w, dims, preferred_element_type=jnp.float32)
         up = lax.dot_general(layer_normed, up_w, dims, preferred_element_type=jnp.float32)

time: 1050 us -> 991 us (0.944)
  waiting for transfers between devices: 862 us -> 573 us
  blocking collectives: 67.3 us -> 299 us
    all_gather x4 -> x0, waiting for transfers between devices: 289 us -> none  [on_device(): whole = lax.all_gather(current, 'fsdp', axis=2, tiled=True)]
    all_to_all x0 -> x4, blocking collectives: none -> 231 us  [open_sectors_for(): lax.all_to_all(jnp.stack(lax.axis_size('fsdp') * [my_tile], axis=0), axis...]
    reshape x4 -> x0, local copies, waits for them, and re-layouts: 11 us -> none  [on_device(): layer_normed = rms_scaled(whole, gain).reshape(-1, width)]
  transfers between devices with their start and end apart: 11 -> 7, of which waited for: 11 -> 7; matrix products, arithmetic and copies ran while one was open for 0% -> 0% of each run, Pallas kernels for 0% -> 0%
where the time goes in v1:
time: 991 us; the launch traced here: 986 us
  waiting for transfers between devices  573 us (58%)
  blocking collectives  299 us (30%)
  matrix products  35.3 us (4%)
  other arithmetic  31.6 us (3%)
  local copies, waits for them, and re-layouts  22.8 us (2%)
  between operations  13.8 us (1%)
  starting transfers between devices  10.3 us (1%)
    reduce_scatter x4, waiting for transfers between devices, on_device(): lax.psum_scatter(partial_sum, 'fsdp', scatter_dimension=2, tiled=True)  568 us
    all_to_all x4, blocking collectives, open_sectors_for(): lax.all_to_all(jnp.stack(lax.axis_size('fsdp') * [my_tile], axis=0), axis...  231 us
    all_gather x1, blocking collectives, on_device(): lax.all_gather(audio_ln, 'fsdp', axis=0, tiled=True)  50.3 us
  transfers between devices with their start and end apart: 7, of which 7 were waited for; matrix products, arithmetic and copies ran while one was open for 0% of the time, Pallas kernels for 0%

profile of v1, /device:TPU:8, one launch (start us, length us, event | category | flops | bytes accessed | tf_op | source)
XLA Modules:
  0.0 985.6 jit_solution(11656536664478741694)
XLA Ops:
  8.4 50.3 %all-gather = bf16[64,2,1280]{2,1,0:T(2,128)(2,1)S(1)} all-gather(bf16[1,2,1280]{2,1,0:T(2,128)(2,1)S(1)} %fusion.112), channel_id=1, replica_groups=mesh['section'=4,'fsdp'=64] {'fsdp'}, dimensions={0}, use_global_device_ids=true | all-gather | bytes 332800 | tf_op jit(solution)/shard_map/all_gather | solution.py:52
  66.6 57.5 %all_to_all.20 = bf16[64,64,2,128]{3,2,1,0:T(2,128)(2,1)S(1)} all-to-all(bf16[64,64,2,128]{3,2,1,0:T(2,128)(2,1)S(1)} %stack.8), channel_id=1, replica_groups=mesh['section'=4,'fsdp'=64] {'fsdp'}, dimensions={0} | all-to-all | bytes 4194304 | tf_op jit(solution)/shard_map/all_to_all | solution.py:85
  126.5 3.9 fusion.39
  130.4 2.4 copy.110
  136.9 4.8 fusion.18
  141.8 141.4 %reduce-scatter.5.cloned.1.call-done = f32[64,2,128]{2,0,1:T(8,128)} async-done(((f32[64,2,8192]{2,0,1:T(8,128)}), f32[64,2,128]{2,0,1:T(8,128)}) %reduce-scatter.5.cloned.1.call-update) | async-done | bytes 65552 | tf_op jit(solution)/shard_map/reduce_scatter | solution.py:101
  284.0 3.4 collective-permute-start
  291.1 58.1 %all_to_all.21 = bf16[64,64,2,128]{3,2,1,0:T(2,128)(2,1)S(1)} all-to-all(bf16[64,64,2,128]{3,2,1,0:T(2,128)(2,1)S(1)} %stack.9), channel_id=1, replica_groups=mesh['section'=4,'fsdp'=64] {'fsdp'}, dimensions={0} | all-to-all | bytes 4194304 | tf_op jit(solution)/shard_map/all_to_all | solution.py:85
  351.5 3.9 fusion.38
  355.4 2.4 copy.116
  361.9 4.8 fusion.16
  366.8 142.3 %reduce-scatter.7.cloned.1.call-done = f32[64,2,128]{2,0,1:T(8,128)} async-done(((f32[64,2,8192]{2,0,1:T(8,128)}), f32[64,2,128]{2,0,1:T(8,128)}) %reduce-scatter.7.cloned.1.call-update) | async-done | bytes 65552 | tf_op jit(solution)/shard_map/reduce_scatter | solution.py:101
  509.9 3.4 collective-permute-start.1
  517.0 57.9 %all_to_all.22 = bf16[64,64,2,128]{3,2,1,0:T(2,128)(2,1)S(1)} all-to-all(bf16[64,64,2,128]{3,2,1,0:T(2,128)(2,1)S(1)} %stack.10), channel_id=1, replica_groups=mesh['section'=4,'fsdp'=64] {'fsdp'}, dimensions={0} | all-to-all | bytes 4194304 | tf_op jit(solution)/shard_map/all_to_all | solution.py:85
  577.2 3.9 fusion.37
  581.1 2.4 copy.122
  587.6 4.8 fusion.14
  592.5 142.2 %reduce-scatter.9.cloned.1.call-done = f32[64,2,128]{2,0,1:T(8,128)} async-done(((f32[64,2,8192]{2,0,1:T(8,128)}), f32[64,2,128]{2,0,1:T(8,128)}) %reduce-scatter.9.cloned.1.call-update) | async-done | bytes 65552 | tf_op jit(solution)/shard_map/reduce_scatter | solution.py:101
  735.6 3.4 collective-permute-start.2
  742.6 57.9 %all_to_all.23 = bf16[64,64,2,128]{3,2,1,0:T(2,128)(2,1)S(1)} all-to-all(bf16[64,64,2,128]{3,2,1,0:T(2,128)(2,1)S(1)} %stack.11), channel_id=1, replica_groups=mesh['section'=4,'fsdp'=64] {'fsdp'}, dimensions={0} | all-to-all | bytes 4194304 | tf_op jit(solution)/shard_map/all_to_all | solution.py:85
  802.8 3.9 fusion.36
  813.2 4.8 fusion.12
  818.1 142.3 %reduce-scatter.11.cloned.1.call-done = f32[64,2,128]{2,0,1:T(8,128)} async-done(((f32[64,2,8192]{2,0,1:T(8,128)}), f32[64,2,128]{2,0,1:T(8,128)}) %reduce-scatter.11.cloned.1.call-update) | async-done | bytes 65552 | tf_op jit(solution)/shard_map/reduce_scatter | solution.py:101
  961.2 17.0 %psum.7 = bf16[64,2,128]{2,0,1:T(8,128)(2,1)S(1)} all-reduce(bf16[64,2,128]{2,0,1:T(8,128)(2,1)S(1)} %fusion.101), channel_id=1, replica_groups=mesh['section'=4,'fsdp'=64] {'section'}, use_global_device_ids=true, to_apply=%region_12.13 | all-reduce | flops 16384 | bytes 65536 | tf_op jit(solution)/shard_map/psum | solution.py:15
  (94 shorter events, 52.4 us)
Async XLA Ops:
  6.5 55.3 %copy-start = (bf16[1280,128]{1,0:T(8,128)(2,1)S(1)}, bf16[1280,128]{1,0:T(8,128)(2,1)}, u32[]{:S(2)}) copy-start(bf16[1280,128]{1,0:T(8,128)(2,1)} %param.21) | copy-start | bytes 983044
  6.5 276.7 %reduce-scatter.5.cloned.1.call-start = ((), (), s32[]{:S(2)}) async-start(), calls=%async_computation.8 | async-start | bytes 4259840 | tf_op jit(solution)/shard_map/reduce_scatter | solution.py:101
  64.6 61.9 %copy-start.1 = (f32[1,8192]{1,0:T(1,128)S(1)}, f32[1,8192]{1,0:T(1,128)}, u32[]{:S(2)}) copy-start(f32[1,8192]{1,0:T(1,128)} %param.24) | copy-start | bytes 98308
  126.4 6.4 copy-start.2
  132.8 2.1 copy-start.6
  141.7 367.4 %reduce-scatter.7.cloned.1.call-start = ((), (), s32[]{:S(2)}) async-start(), calls=%async_computation.9 | async-start | bytes 4259840 | tf_op jit(solution)/shard_map/reduce_scatter | solution.py:101
  284.0 5.0 collective-permute-start
  351.5 6.4 copy-start.3
  357.9 2.1 copy-start.7
  366.8 367.9 %reduce-scatter.9.cloned.1.call-start = ((), (), s32[]{:S(2)}) async-start(), calls=%async_computation.10 | async-start | bytes 4259840 | tf_op jit(solution)/shard_map/reduce_scatter | solution.py:101
  509.9 5.0 collective-permute-start.1
  577.2 6.4 copy-start.4
  583.5 2.1 copy-start.8
  592.4 367.9 %reduce-scatter.11.cloned.1.call-start = ((), (), s32[]{:S(2)}) async-start(), calls=%async_computation.11 | async-start | bytes 4259840 | tf_op jit(solution)/shard_map/reduce_scatter | solution.py:101
  735.6 5.0 collective-permute-start.2
  802.8 6.4 copy-start.5
  809.2 2.1 copy-start.9
Sparse Core Ops, SparseCore 0:
  141.8 141.3 reduce-scatter.4
  366.9 142.1 reduce-scatter.6
  592.6 142.0 reduce-scatter.8
  818.2 142.1 reduce-scatter.10
